TPU v7x, 32 devices: a whole 2x2x4 slice. The times are simulated.
32 devices in a mesh: dp: 2 (over x), fsdp: 2 (over core), tensor: 8 (over z, y).
Axes of the slice: x: 2, y: 2, z: 4, core: 2. Of those that a mesh axis runs over, the one named last changes fastest.
Arguments:
- weight: float32 [4096, 8192], P('fsdp', 'tensor'), may hold values from -6 to 6
- momentum: float32 [4096, 8192], P('fsdp', 'tensor'), may hold values from -180 to 180
- right_basis: float32 [256, 8192], P('fsdp', 'tensor'), may hold values from -0.0625 to 0.0625
- gradients: bfloat16 [1, 2, 4096, 8192], P(None, 'dp', 'fsdp', 'tensor'), may hold values from -6 to 6
Outputs:
- new_weight: float32 [4096, 8192], P('fsdp', 'tensor')
- new_momentum: float32 [4096, 8192], P('fsdp', 'tensor')
- new_basis: float32 [256, 8192], P('fsdp', 'tensor')
All inputs are finite; a program needn't handle non-finite values.
Results may differ from a plain program's by a relative error of at most 0.0003.
Values sent between devices are 32-bit elements; how exact they have to be, the bound alone decides.
A program may use at most 128 MiB of HBM per device.

v0:
```python
import math

import jax
import jax.numpy as jnp
from jax import lax
from jax.sharding import PartitionSpec as P

D = 8192
ROWS = 4096
RANK = 256


highest = lax.Precision.HIGHEST
step_size = 0.3
drop_share = 0.05
guard_term = 1e-06


def contract(left, right, left_dim, right_dim):
    return lax.dot_general(
        left,
        right,
        (((left_dim,), (right_dim,)), ((), ())),
        precision=highest,
        preferred_element_type=jnp.float32,
    )


def sketch_term(momentum, pieces):
    return contract(momentum, pieces, 1, 1)


def coefficient_term(left_basis, momentum):
    return contract(left_basis, momentum, 0, 0)


def column_scale(coefficients):
    squares = lax.psum(jnp.sum(coefficients * coefficients, axis=1), "tensor")
    return lax.rsqrt(squares + guard_term)


def grad_whole(gradient):
    return lax.psum(gradient, "dp")


def gram_rows(gram_matrix):
    return lax.psum(gram_matrix, "fsdp")


def coef_rows(left_basis, momentum):
    coefficients = lax.psum_scatter(
        coefficient_term(left_basis, momentum), "fsdp", scatter_dimension=0, tiled=True
    )
    inverse = column_scale(coefficients)
    return (
        lax.all_gather(coefficients, "fsdp", axis=0, tiled=True),
        lax.all_gather(inverse, "fsdp", axis=0, tiled=True),
    )


def solve_rows(gram_matrix, sketch):
    lower_factor = jnp.linalg.cholesky(gram_matrix)
    return lax.linalg.triangular_solve(
        lower_factor, sketch, left_side=False, lower=True, transpose_a=True
    )


def run_steps(weight, momentum, right_basis, gradients, grad_sum, gram_sum, coef_sum):
    step_scale = step_size * math.sqrt(ROWS * D / RANK)
    momentum = momentum + grad_sum(gradients[0, 0].astype(jnp.float32))
    sketch_part = sketch_term(momentum, lax.all_gather(right_basis, "fsdp", axis=0, tiled=True))
    sketch = lax.psum(sketch_part, "tensor")
    gram_matrix = gram_sum(contract(sketch, sketch, 0, 0))
    left_basis = solve_rows(gram_matrix, sketch)
    coefficients, inverse = coef_sum(left_basis, momentum)
    right_basis = coefficients * inverse[:, None]
    momentum = momentum - drop_share * contract(left_basis, coefficients, 1, 0)
    weight = weight - step_scale * contract(left_basis, right_basis, 1, 0)
    return (weight, momentum, right_basis)


def shards(weight, momentum, right_basis, gradients):
    share_rows = right_basis.shape[0]
    weight, momentum, right_basis = run_steps(
        weight, momentum, right_basis, gradients, grad_whole, gram_rows, coef_rows
    )
    first_rank = lax.axis_index("fsdp") * share_rows
    return (weight, momentum, lax.dynamic_slice_in_dim(right_basis, first_rank, share_rows, 0))


def solution(mesh):
    return jax.shard_map(
        shards,
        mesh=mesh,
        in_specs=(
            P("fsdp", "tensor"),
            P("fsdp", "tensor"),
            P("fsdp", "tensor"),
            P(None, "dp", "fsdp", "tensor"),
        ),
        out_specs=(P("fsdp", "tensor"), P("fsdp", "tensor"), P("fsdp", "tensor")),
        check_vma=False,
    )
```

profile of v0, /device:TPU:0, one launch (start us, length us, event | category | flops | bytes accessed | tf_op | source)
XLA Modules:
  0.0 507.3 jit_solution(10673599151531180017)
XLA Ops:
  8.0 0.0 all-reduce.5.cloned.1.call-start
  8.0 6.6 %bitcast_convert_fusion = f32[2048,1024]{1,0:T(8,128)} fusion(bf16[1,1,2048,1024]{3,2,1,0:T(8,128)(2,1)} %param.7), kind=kLoop, calls=%fused_computation.4 | loop fusion | flops 2097152 | bytes 12582912 | tf_op jit(solution)/shard_map/convert_element_type | solution.py:70
  14.7 0.0 all-reduce.5.cloned.1.call-update
  14.7 0.0 all-gather.4.cloned.1.call-start
  14.8 0.5 all-gather.4.cloned.1.call-update
  15.3 0.0 all-reduce.7.cloned.1.call-start
  15.3 200.2 %all-reduce.5.cloned.1.call-done = f32[2048,1024]{1,0:T(8,128)} async-done(((f32[2048,1024]{1,0:T(8,128)}), f32[2048,1024]{1,0:T(8,128)}) %all-reduce.5.cloned.1.call-update) | async-done | bytes 8388624 | tf_op jit(solution)/shard_map/psum | solution.py:43
  215.6 12.1 %add.44 = f32[2048,1024]{1,0:T(8,128)} add(f32[2048,1024]{1,0:T(8,128)} %param.5, f32[2048,1024]{1,0:T(8,128)} %all-reduce.5.cloned.1.call-done) | non-fusion elementwise | flops 2097152 | bytes 25165824 | tf_op jit(solution)/shard_map/add | solution.py:70
  227.7 0.0 all-gather.4.cloned.1.call-done
  227.7 10.4 %fusion.13 = f32[2048,256]{1,0:T(8,128)} fusion(f32[2048,1024]{1,0:T(8,128)} %add.44, f32[256,1024]{1,0:T(8,128)} %all-gather.4.cloned.1.call-done), kind=kOutput, calls=%fused_computation.40 | convolution fusion | flops 6442450944 | bytes 11534336 | tf_op jit(solution)/shard_map/dot_general | solution.py:20
  238.1 0.0 all-reduce.7.cloned.1.call-update
  238.1 0.0 all-reduce.9.cloned.1.call-start
  238.2 102.5 %all-reduce.7.cloned.1.call-done = f32[2048,256]{1,0:T(8,128)} async-done(((f32[2048,256]{1,0:T(8,128)}), f32[2048,256]{1,0:T(8,128)}) %all-reduce.7.cloned.1.call-update) | async-done | bytes 2097168 | tf_op jit(solution)/shard_map/psum | solution.py:72
  340.7 0.0 copy-start
  340.7 6.5 %fusion.14 = f32[256,256]{0,1:T(8,128)} fusion(f32[2048,256]{1,0:T(8,128)} %all-reduce.7.cloned.1.call-done), kind=kOutput, calls=%fused_computation.41 | convolution fusion | flops 1610612736 | bytes 2359296 | tf_op jit(solution)/shard_map/dot_general | solution.py:20
  347.2 0.0 all-reduce.9.cloned.1.call-update
  347.2 0.2 reduce-scatter.2.cloned.1.call-start
  347.5 17.0 %all-reduce.9.cloned.1.call-done = f32[256,256]{0,1:T(8,128)} async-done(((f32[256,256]{0,1:T(8,128)}), f32[256,256]{0,1:T(8,128)}) %all-reduce.9.cloned.1.call-update) | async-done | bytes 262160 | tf_op jit(solution)/shard_map/psum | solution.py:47
  364.5 1.1 copy.10
  365.6 1.0 fusion.3
  366.6 11.7 %cholesky.50 = f32[128,128]{1,0:T(8,128)S(1)} custom-call(f32[128,128]{1,0:T(8,128)S(1)} %cholesky.118), custom_call_target="Cholesky" | custom-call | tf_op jit(solution)/shard_map/jit(cholesky)/cholesky | solution.py:62
  378.3 9.8 %custom-call.14 = f32[1,128,128]{1,2,0:T(8,128)S(1)} custom-call(f32[1,128,128]{2,1,0:T(8,128)S(1)} %get-tuple-element.24), custom_call_target="InvertDiagBlocksLowerTriangular" | custom-call | tf_op jit(solution)/shard_map/jit(cholesky)/cholesky | solution.py:62
  388.1 0.2 constant_dynamic-update-slice_fusion
  388.4 0.3 convolution_subtract_fusion.1
  388.6 11.7 %cholesky.105 = f32[128,128]{1,0:T(8,128)S(1)} custom-call(f32[128,128]{1,0:T(8,128)S(1)} %convolution_subtract_fusion.1), custom_call_target="Cholesky" | custom-call | tf_op jit(solution)/shard_map/jit(cholesky)/cholesky | solution.py:62
  400.4 0.7 compare_reduce_fusion
  402.4 0.1 triangular_solve.58
  402.4 4.1 while.1
  402.6 0.6 fusion.27
  403.2 1.3 bitcast_dynamic-update-slice_fusion.2
  404.6 0.6 fusion.27
  405.2 1.3 bitcast_dynamic-update-slice_fusion.2
  406.5 19.7 %custom-call.15 = f32[2,128,128]{1,2,0:T(8,128)S(1)} custom-call(f32[2,128,128]{2,1,0:T(8,128)S(1)} %get-tuple-element.10), custom_call_target="InvertDiagBlocksLowerTriangular" | custom-call | tf_op jit(solution)/shard_map/triangular_solve | solution.py:63
  426.2 0.0 copy-done
  426.2 1.1 fusion.1
  427.3 1.8 convolution_subtract_fusion
  429.1 1.1 fusion.4
  430.2 10.4 %fusion = f32[256,1024]{1,0:T(8,128)} fusion(f32[2048,1024]{1,0:T(8,128)} %add.44, f32[2048,128]{0,1:T(8,128)S(1)} %fusion.4, f32[2048,128]{0,1:T(8,128)S(1)} %fusion.1), kind=kOutput, calls=%fused_computation.7 | convolution fusion | flops 6442975232 | bytes 11534336 | tf_op jit(solution)/shard_map/dot_general | solution.py:20
  440.6 0.0 reduce-scatter.2.cloned.1.call-update
  440.6 0.0 all-gather.6.cloned.1.call-start
  440.7 9.7 %reduce-scatter.2.cloned.1.call-done = f32[128,1024]{1,0:T(8,128)} async-done(((f32[256,1024]{1,0:T(8,128)}), f32[128,1024]{1,0:T(8,128)}) %reduce-scatter.2.cloned.1.call-update) | async-done | bytes 524304 | tf_op jit(solution)/shard_map/reduce_scatter | solution.py:51
  450.4 0.0 all-gather.6.cloned.1.call-update
  450.5 1.2 multiply_reduce_fusion
  451.6 21.6 %psum.31 = f32[128]{0:T(128)S(1)} all-reduce(f32[128]{0:T(128)S(1)} %multiply_reduce_fusion), channel_id=1, replica_groups=mesh['dp'=2,'fsdp'=2,'tensor'=8] {'tensor'}, use_global_device_ids=true, to_apply=%region_9.10 | all-reduce | flops 128 | bytes 1024 | tf_op jit(solution)/shard_map/psum | solution.py:38
  473.2 1.8 all-gather
  475.0 0.0 all-gather.6.cloned.1.call-done
  475.0 0.0 slice-start
  475.0 1.5 broadcast_multiply_fusion
  476.5 0.0 slice-start.1
  476.5 0.0 copy-start.1
  476.5 12.1 %multiply_subtract_fusion.1 = f32[2048,1024]{1,0:T(8,128)} fusion(f32[2048,1024]{1,0:T(8,128)} %param.4, f32[256,1024]{1,0:T(8,128)S(1)} %broadcast_multiply_fusion, f32[2048,128]{0,1:T(8,128)S(1)} %fusion.4, f32[2048,128]{0,1:T(8,128)S(1)} %fusion.1), kind=kOutput, calls=%fused_computation.3 | convolution fusion | flops 6447169536 | bytes 19922944 | tf_op jit(solution)/shard_map/dot_general | solution.py:20
  488.6 0.8 constant_dynamic-slice_fusion.1
  489.4 0.0 slice-done
  489.4 0.0 slice-done.1
  489.4 0.0 copy-done.1
  489.4 9.8 %multiply_subtract_fusion = f32[2048,1024]{1,0:T(8,128)} fusion(f32[2048,1024]{1,0:T(8,128)S(1)} %bitcast.45, f32[256,1024]{1,0:T(8,128)S(1)} %copy-done.1, f32[2048,128]{0,1:T(8,128)S(1)} %fusion.4, f32[2048,128]{0,1:T(8,128)S(1)} %fusion.1), kind=kOutput, calls=%fused_computation.2 | convolution fusion | flops 6447169536 | bytes 19922944 | tf_op jit(solution)/shard_map/dot_general | solution.py:20
  (11 shorter events, 0.2 us)
Async XLA Ops:
  8.0 207.6 %all-reduce.5.cloned.1.call-start = ((), (), s32[]{:S(2)}) async-start(), calls=%async_computation.1 | async-start | bytes 16777216 | tf_op jit(solution)/shard_map/psum | solution.py:43
  14.7 213.0 %all-gather.4.cloned.1.call-start = ((), (), s32[]{:S(2)}) async-start(), calls=%async_computation.2 | async-start | bytes 1572864 | tf_op jit(solution)/shard_map/all_gather | solution.py:71
  15.3 325.4 %all-reduce.7.cloned.1.call-start = ((), (), s32[]{:S(2)}) async-start(), calls=%async_computation.3 | async-start | bytes 4194304 | tf_op jit(solution)/shard_map/psum | solution.py:72
  238.1 126.4 %all-reduce.9.cloned.1.call-start = ((), (), s32[]{:S(2)}) async-start(), calls=%async_computation.4 | async-start | bytes 524288 | tf_op jit(solution)/shard_map/psum | solution.py:47
  340.7 85.6 %copy-start = (f32[2048,256]{1,0:T(8,128)S(1)}, f32[2048,256]{1,0:T(8,128)}, u32[]{:S(2)}) copy-start(f32[2048,256]{1,0:T(8,128)} %all-reduce.7.cloned.1.call-done) | copy-start | bytes 6291460
  347.2 103.2 %reduce-scatter.2.cloned.1.call-start = ((), (), s32[]{:S(2)}) async-start(), calls=%async_computation.5 | async-start | bytes 1572864 | tf_op jit(solution)/shard_map/reduce_scatter | solution.py:51
  440.6 34.4 %all-gather.6.cloned.1.call-start = ((), (), s32[]{:S(2)}) async-start(), calls=%async_computation.6 | async-start | bytes 1572864 | tf_op jit(solution)/shard_map/all_gather | solution.py:56
  475.0 14.4 %slice-start = ((s8[8388608]{0:T(1024)(128)(4,1)}), s8[4194304]{0:T(1024)(128)(4,1)S(1)}, s32[]{:S(2)}) async-start(s8[8388608]{0:T(1024)(128)(4,1)} %bitcast.44), calls=%async_computation.7 | async-start | bytes 8388608
  476.5 12.9 %slice-start.1 = ((s8[8388608]{0:T(1024)(128)(4,1)}), s8[4194304]{0:T(1024)(128)(4,1)S(1)}, s32[]{:S(2)}) async-start(s8[8388608]{0:T(1024)(128)(4,1)} %bitcast.44), calls=%async_computation.8 | async-start | bytes 8388608
  476.5 12.9 %copy-start.1 = (f32[256,1024]{1,0:T(8,128)S(1)}, f32[256,1024]{1,0:T(8,128)}, u32[]{:S(2)}) copy-start(f32[256,1024]{1,0:T(8,128)} %all-gather.6.cloned.1.call-done) | copy-start | bytes 3145732
Sparse Core Ops, SparseCore 0:
  14.8 200.7 all-reduce.4
Sparse Core Ops, SparseCore 1:
  16.7 11.6 all-gather.3
  238.2 102.4 all-reduce.6
  347.3 17.1 all-reduce.8
  440.7 9.7 reduce-scatter.1
  452.0 10.0 all-gather.5
where the time goes:
time: 515 us; the launch traced here: 507 us
  waiting for transfers between devices  330 us (64%)
  other arithmetic  76.1 us (15%)
  matrix products  53.6 us (10%)
  blocking collectives  23.4 us (5%)
  between operations  17.5 us (3%)
  local copies, waits for them, and re-layouts  5.89 us (1%)
    psum x1, waiting for transfers between devices, grad_whole(): return lax.psum(gradient, 'dp')  200 us
    psum x1, waiting for transfers between devices, run_steps(): sketch = lax.psum(sketch_part, 'tensor')  103 us
    dot_general x5, matrix products, contract(): lax.dot_general(left, right, (((left_dim,), (right_dim,)), ((), ())), pre...  49.2 us
    another operation x6, other arithmetic, solve_rows(): lower_factor = jnp.linalg.cholesky(gram_matrix)  34 us
    psum x1, blocking collectives, column_scale(): squares = lax.psum(jnp.sum(coefficients * coefficients, axis=1), 'tensor')  21.6 us
    another operation x3, other arithmetic, solve_rows(): lax.linalg.triangular_solve(lower_factor, sketch, left_side=False, lower=...  19.7 us
    psum x1, waiting for transfers between devices, gram_rows(): return lax.psum(gram_matrix, 'fsdp')  17 us
    add x1, other arithmetic, run_steps(): momentum = momentum + grad_sum(gradients[0, 0].astype(jnp.float32))  12.1 us
  transfers between devices with their start and end apart: 6, of which 4 were waited for; matrix products, arithmetic and copies ran while one was open for 3% of the time, Pallas kernels for 0%

commit v1 on v0

v1 whole, which is shorter than its diff:
```python
import math

import jax
import jax.numpy as jnp
from jax import lax
from jax.sharding import PartitionSpec as P

highest = lax.Precision.HIGHEST
step_size = 0.3
drop_share = 0.05
guard_term = 1e-06


def contract(left, right, left_dim, right_dim):
    return lax.dot_general(
        left,
        right,
        (((left_dim,), (right_dim,)), ((), ())),
        precision=highest,
        preferred_element_type=jnp.float32,
    )


def inverse_factor(gram):
    lower = jnp.linalg.cholesky(gram)
    eye = jnp.eye(gram.shape[0], dtype=jnp.float32)
    return lax.linalg.triangular_solve(lower, eye, left_side=True, lower=True)


def shards(n_dp, step_scale, weight, momentum, right_basis, gradients):
    share_rows = right_basis.shape[0]
    gradient = gradients[0, 0].astype(jnp.float32)
    other = lax.ppermute(gradient, "dp", [(i, (i + 1) % n_dp) for i in range(n_dp)])
    basis = lax.all_gather(right_basis, "fsdp", axis=0, tiled=True)
    share = momentum * (1.0 / n_dp) + gradient
    part = contract(share, basis, 1, 1)
    block = lax.psum_scatter(part, "tensor", scatter_dimension=0, tiled=True)
    block = lax.psum(block, "dp")
    gram = lax.psum(contract(block, block, 0, 0), ("tensor", "fsdp"))
    sketch = lax.all_gather(block, "tensor", axis=0, tiled=True)
    inverse = inverse_factor(gram)
    product = lax.psum_scatter(contract(sketch, share, 0, 0), "fsdp", scatter_dimension=0, tiled=True)
    product = lax.all_gather(lax.psum(product, "dp"), "fsdp", axis=0, tiled=True)
    coefficients = contract(inverse, product, 1, 0)
    left_basis = contract(sketch, inverse, 1, 1)
    squares = lax.psum(jnp.sum(coefficients * coefficients, axis=1), "tensor")
    scale = lax.rsqrt(squares + guard_term)
    scaled = coefficients * scale[:, None]
    weight = weight - step_scale * contract(left_basis, scaled, 1, 0)
    total = momentum + (gradient + other)
    momentum = total - drop_share * contract(left_basis, coefficients, 1, 0)
    first_rank = lax.axis_index("fsdp") * share_rows
    return weight, momentum, lax.dynamic_slice_in_dim(scaled, first_rank, share_rows, 0)


def solution(mesh):
    n_dp = mesh.shape["dp"]

    def step(weight, momentum, right_basis, gradients):
        rows, width = weight.shape
        step_scale = step_size * math.sqrt(rows * width / right_basis.shape[0])

        def local(*blocks):
            return shards(n_dp, step_scale, *blocks)

        return jax.shard_map(
            local,
            mesh=mesh,
            in_specs=(
                P("fsdp", "tensor"),
                P("fsdp", "tensor"),
                P("fsdp", "tensor"),
                P(None, "dp", "fsdp", "tensor"),
            ),
            out_specs=(P("fsdp", "tensor"), P("fsdp", "tensor"), P("fsdp", "tensor")),
            check_vma=False,
        )(weight, momentum, right_basis, gradients)

    return step
```

time: 515 us -> 420 us (0.82); the launches traced: 507 us -> 420 us
  waiting for transfers between devices: 330 us -> 258 us
  other arithmetic: 76.1 us -> 61.5 us
    psum x3, waiting for transfers between devices: 320 us -> 132 us  [the longest x1 78.8 us: shards(): gram = lax.psum(contract(block, block, 0, 0), ('tensor', 'fsdp'))]
    reduce_scatter x1 -> x2, waiting for transfers between devices: 9.74 us -> 69.1 us  [the longest x1 69.1 us: shards(): block = lax.psum_scatter(part, 'tensor', scatter_dimension=0, tiled=True)]
    all_gather x2 -> x3, waiting for transfers between devices: 0.01 us -> 56.5 us  [the longest x1 43.1 us: shards(): sketch = lax.all_gather(block, 'tensor', axis=0, tiled=True)]
    add x1 -> x0, other arithmetic: 12.1 us -> none  [run_steps(): momentum = momentum + grad_sum(gradients[0, 0].astype(jnp.float32))]
    dot_general x5 -> x7, matrix products: 49.2 us -> 54.7 us  [contract(): lax.dot_general(left, right, (((left_dim,), (right_dim,)), ((), ())), pre...]
  transfers between devices with their start and end apart: 6 -> 9, of which waited for: 4 -> 6; matrix products, arithmetic and copies ran while one was open for 3% -> 24% of each run, Pallas kernels for 0% -> 0%
where the time goes in v1:
time: 420 us
  waiting for transfers between devices  258 us (61%)
  other arithmetic  61.5 us (15%)
  matrix products  56 us (13%)
  blocking collectives  21.4 us (5%)
  between operations  15.6 us (4%)
  local copies, waits for them, and re-layouts  5.98 us (1%)
    psum x1, waiting for transfers between devices, shards(): gram = lax.psum(contract(block, block, 0, 0), ('tensor', 'fsdp'))  78.8 us
    reduce_scatter x1, waiting for transfers between devices, shards(): block = lax.psum_scatter(part, 'tensor', scatter_dimension=0, tiled=True)  69.1 us
    dot_general x7, matrix products, contract(): lax.dot_general(left, right, (((left_dim,), (right_dim,)), ((), ())), pre...  54.7 us
    all_gather x1, waiting for transfers between devices, shards(): sketch = lax.all_gather(block, 'tensor', axis=0, tiled=True)  43.1 us
    another operation x6, other arithmetic, inverse_factor(): lower = jnp.linalg.cholesky(gram)  33.9 us
    psum x1, waiting for transfers between devices, shards(): lax.psum(product, 'dp')  28.7 us
    psum x1, waiting for transfers between devices, shards(): block = lax.psum(block, 'dp')  24.5 us
    psum x1, blocking collectives, shards(): squares = lax.psum(jnp.sum(coefficients * coefficients, axis=1), 'tensor')  21.4 us
  transfers between devices with their start and end apart: 9, of which 6 were waited for; matrix products, arithmetic and copies ran while one was open for 24% of the time, Pallas kernels for 0%

profile of v1, /device:TPU:0, one launch (start us, length us, event | category | flops | bytes accessed | tf_op | source)
XLA Modules:
  0.0 419.9 jit_solution(3459437659978223350)
XLA Ops:
  7.2 0.0 all-gather.4.cloned.1.call-start
  7.2 0.7 all-gather.4.cloned.1.call-update
  7.9 0.0 reduce-scatter.3.cloned.1.call-start
  7.9 13.4 %all-gather.4.cloned.1.call-done = f32[256,1024]{1,0:T(8,128)} async-done(((f32[128,1024]{1,0:T(8,128)}), f32[256,1024]{1,0:T(8,128)}) %all-gather.4.cloned.1.call-update) | async-done | bytes 1048592 | tf_op jit(solution)/shard_map/all_gather | solution.py:34
  21.3 11.2 %fusion.1 = f32[2048,256]{1,0:T(8,128)} fusion(f32[256,1024]{1,0:T(8,128)} %all-gather.4.cloned.1.call-done, f32[2048,1024]{1,0:T(8,128)} %param.5, bf16[1,1,2048,1024]{3,2,1,0:T(8,128)(2,1)} %param.7), kind=kOutput, calls=%fused_computation.6 | convolution fusion | flops 6448742400 | bytes 15728640 | tf_op jit(solution)/shard_map/dot_general | solution.py:15
  32.5 0.0 reduce-scatter.3.cloned.1.call-update
  32.5 0.0 all-reduce.5.cloned.1.call-start
  32.6 69.1 %reduce-scatter.3.cloned.1.call-done = f32[256,256]{1,0:T(8,128)} async-done(((f32[2048,256]{1,0:T(8,128)}), f32[256,256]{1,0:T(8,128)}) %reduce-scatter.3.cloned.1.call-update) | async-done | bytes 262160 | tf_op jit(solution)/shard_map/reduce_scatter | solution.py:37
  101.7 0.0 all-reduce.5.cloned.1.call-update
  101.7 0.0 all-gather.6.cloned.1.call-start
  101.8 24.5 %all-reduce.5.cloned.1.call-done = f32[256,256]{1,0:T(8,128)} async-done(((f32[256,256]{1,0:T(8,128)}), f32[256,256]{1,0:T(8,128)}) %all-reduce.5.cloned.1.call-update) | async-done | bytes 262160 | tf_op jit(solution)/shard_map/psum | solution.py:38
  126.2 0.0 copy-start.1
  126.2 0.0 all-gather.6.cloned.1.call-update
  126.2 0.0 all-reduce.7.cloned.1.call-start
  126.3 6.7 %bitcast_convert_fusion = f32[2048,1024]{1,0:T(8,128)} fusion(bf16[1,1,2048,1024]{3,2,1,0:T(8,128)(2,1)} %param.7), kind=kLoop, calls=%fused_computation.9 | loop fusion | flops 2097152 | bytes 12582912 | tf_op jit(solution)/shard_map/convert_element_type | solution.py:32
  133.0 0.3 collective-permute-start
  133.2 0.0 copy-done.1
  133.2 1.3 fusion.21
  134.5 0.0 all-reduce.7.cloned.1.call-update
  134.5 0.0 reduce-scatter.5.cloned.1.call-start
  134.6 43.1 %all-gather.6.cloned.1.call-done = f32[2048,256]{1,0:T(8,128)} async-done(((f32[256,256]{1,0:T(8,128)}), f32[2048,256]{1,0:T(8,128)}) %all-gather.6.cloned.1.call-update) | async-done | bytes 2097168 | tf_op jit(solution)/shard_map/all_gather | solution.py:40
  177.7 12.4 %fusion = f32[256,1024]{1,0:T(8,128)} fusion(f32[2048,256]{1,0:T(8,128)} %all-gather.6.cloned.1.call-done, f32[2048,1024]{1,0:T(8,128)} %param.5, bf16[1,1,2048,1024]{3,2,1,0:T(8,128)(2,1)} %param.7), kind=kOutput, calls=%fused_computation.5 | convolution fusion | flops 6448742400 | bytes 15728640 | tf_op jit(solution)/shard_map/dot_general | solution.py:15
  190.1 0.0 reduce-scatter.5.cloned.1.call-update
  190.1 0.2 all-reduce.9.cloned.1.call-start
  190.4 78.8 %all-reduce.7.cloned.1.call-done = f32[256,256]{0,1:T(8,128)} async-done(((f32[256,256]{0,1:T(8,128)}), f32[256,256]{0,1:T(8,128)}) %all-reduce.7.cloned.1.call-update) | async-done | bytes 262160 | tf_op jit(solution)/shard_map/psum | solution.py:39
  269.2 1.1 copy.8
  270.3 1.0 fusion.6
  271.3 11.7 %cholesky.50 = f32[128,128]{1,0:T(8,128)S(1)} custom-call(f32[128,128]{1,0:T(8,128)S(1)} %cholesky.118), custom_call_target="Cholesky" | custom-call | tf_op jit(solution)/shard_map/jit(cholesky)/cholesky | solution.py:25
  283.1 9.8 %custom-call.14 = f32[1,128,128]{1,2,0:T(8,128)S(1)} custom-call(f32[1,128,128]{2,1,0:T(8,128)S(1)} %get-tuple-element.24), custom_call_target="InvertDiagBlocksLowerTriangular" | custom-call | tf_op jit(solution)/shard_map/jit(cholesky)/cholesky | solution.py:25
  292.9 0.2 constant_dynamic-update-slice_fusion
  293.1 0.3 convolution_subtract_fusion.1
  293.4 11.7 %cholesky.105 = f32[128,128]{1,0:T(8,128)S(1)} custom-call(f32[128,128]{1,0:T(8,128)S(1)} %convolution_subtract_fusion.1), custom_call_target="Cholesky" | custom-call | tf_op jit(solution)/shard_map/jit(cholesky)/cholesky | solution.py:25
  305.1 0.0 reduce-scatter.5.cloned.1.call-done
  305.1 0.0 all-reduce.9.cloned.1.call-update
  305.2 0.3 all-gather.8.cloned.1.call-start
  305.5 0.6 compare_reduce_fusion
  307.5 28.7 %all-reduce.9.cloned.1.call-done = f32[128,1024]{1,0:T(8,128)} async-done(((f32[128,1024]{1,0:T(8,128)}), f32[128,1024]{1,0:T(8,128)}) %all-reduce.9.cloned.1.call-update) | async-done | bytes 524304 | tf_op jit(solution)/shard_map/psum | solution.py:43
  336.1 0.0 all-gather.8.cloned.1.call-update
  336.2 0.1 triangular_solve.63
  336.2 4.0 while.1
  336.2 0.6 fusion.37
  336.8 1.4 bitcast_dynamic-update-slice_fusion.2
  338.2 0.6 fusion.37
  338.8 1.4 bitcast_dynamic-update-slice_fusion.2
  340.2 19.7 %custom-call.15 = f32[2,128,128]{1,2,0:T(8,128)S(1)} custom-call(f32[2,128,128]{2,1,0:T(8,128)S(1)} %get-tuple-element.10), custom_call_target="InvertDiagBlocksLowerTriangular" | custom-call | tf_op jit(solution)/shard_map/triangular_solve | solution.py:27
  359.9 0.3 fusion.9
  360.2 0.3 convolution_subtract_fusion
  360.4 0.3 fusion.12
  360.8 3.4 fusion.8
  364.2 0.0 all-gather.8.cloned.1.call-done
  364.2 2.3 multiply_reduce_fusion
  366.6 21.4 %psum.31 = f32[256]{0:T(256)S(1)} all-reduce(f32[256]{0:T(256)S(1)} %get-tuple-element.27), channel_id=1, replica_groups=mesh['dp'=2,'fsdp'=2,'tensor'=8] {'tensor'}, use_global_device_ids=true, to_apply=%region_10.11 | all-reduce | flops 256 | bytes 2048 | tf_op jit(solution)/shard_map/psum | solution.py:46
  387.9 0.1 broadcast_multiply_fusion
  388.1 0.0 slice-start
  388.1 0.8 constant_dynamic-slice_fusion.1
  388.9 0.0 slice-start.1
  388.9 0.0 copy-start
  388.9 11.8 %multiply_subtract_fusion.1 = f32[2048,1024]{1,0:T(8,128)} fusion(f32[2048,1024]{1,0:T(8,128)} %param.4, f32[2048,256]{1,0:T(8,128)S(1)} %fusion.8, f32[256,1024]{1,0:T(8,128)S(1)} %broadcast_multiply_fusion), kind=kOutput, calls=%fused_computation.3 | convolution fusion | flops 6446645248 | bytes 19922944 | tf_op jit(solution)/shard_map/dot_general | solution.py:15
  400.8 0.0 collective-permute-done
  400.8 0.0 slice-done
  400.8 0.0 slice-done.1
  400.8 0.0 copy-done
  400.8 12.2 %multiply_subtract_fusion = f32[2048,1024]{1,0:T(8,128)} fusion(f32[2048,1024]{1,0:T(8,128)S(1)} %bitcast.54, f32[2048,1024]{1,0:T(8,128)} %collective-permute-done, f32[2048,256]{1,0:T(8,128)S(1)} %fusion.8, f32[256,1024]{1,0:T(8,128)S(1)} %get-tuple-element.28, bf16[1,1,2048,1024]{3,2,1,0:T(8,128)(2,1)S(1)} %copy-done), kind=kOutput, calls=%fused_computation.2 | convolution fusion | flops 6452936704 | bytes 32505856 | tf_op jit(solution)/shard_map/dot_general | solution.py:15
  (12 shorter events, 0.2 us)
Async XLA Ops:
  7.2 14.1 %all-gather.4.cloned.1.call-start = ((), (), s32[]{:S(2)}) async-start(), calls=%async_computation.2 | async-start | bytes 1572864 | tf_op jit(solution)/shard_map/all_gather | solution.py:34
  7.9 93.8 %reduce-scatter.3.cloned.1.call-start = ((), (), s32[]{:S(2)}) async-start(), calls=%async_computation.3 | async-start | bytes 2359296 | tf_op jit(solution)/shard_map/reduce_scatter | solution.py:37
  32.5 93.7 %all-reduce.5.cloned.1.call-start = ((), (), s32[]{:S(2)}) async-start(), calls=%async_computation.4 | async-start | bytes 524288 | tf_op jit(solution)/shard_map/psum | solution.py:38
  101.7 76.0 %all-gather.6.cloned.1.call-start = ((), (), s32[]{:S(2)}) async-start(), calls=%async_computation.5 | async-start | bytes 2359296 | tf_op jit(solution)/shard_map/all_gather | solution.py:40
  126.2 7.0 %copy-start.1 = (f32[256,256]{1,0:T(8,128)S(1)}, f32[256,256]{1,0:T(8,128)}, u32[]{:S(2)}) copy-start(f32[256,256]{1,0:T(8,128)} %all-reduce.5.cloned.1.call-done) | copy-start | bytes 786436
  126.2 143.0 %all-reduce.7.cloned.1.call-start = ((), (), s32[]{:S(2)}) async-start(), calls=%async_computation.6 | async-start | bytes 524288 | tf_op jit(solution)/shard_map/psum | solution.py:39
  133.0 267.8 %collective-permute-start = (f32[2048,1024]{1,0:T(8,128)}, f32[2048,1024]{1,0:T(8,128)}, u32[]{:S(2)}, u32[]{:S(2)}) collective-permute-start(f32[2048,1024]{1,0:T(8,128)} %bitcast_convert_fusion), channel_id=1, source_target_pairs={{0,16},{16,0},{1,17},{17,1},{2,18},{18,2},{3,19},{19,3},{4,20},{20... | collective-permute-start | bytes 25165832 | tf_op jit(solution)/shard_map/ppermute | solution.py:33
  134.5 170.6 %reduce-scatter.5.cloned.1.call-start = ((), (), s32[]{:S(2)}) async-start(), calls=%async_computation.7 | async-start | bytes 1572864 | tf_op jit(solution)/shard_map/reduce_scatter | solution.py:42
  190.1 146.0 %all-reduce.9.cloned.1.call-start = ((), (), s32[]{:S(2)}) async-start(), calls=%async_computation.8 | async-start | bytes 1048576 | tf_op jit(solution)/shard_map/psum | solution.py:43
  305.2 59.0 %all-gather.8.cloned.1.call-start = ((), (), s32[]{:S(2)}) async-start(), calls=%async_computation.9 | async-start | bytes 1572864 | tf_op jit(solution)/shard_map/all_gather | solution.py:43
  388.1 12.7 %slice-start = ((s8[8388608]{0:T(1024)(128)(4,1)}), s8[4194304]{0:T(1024)(128)(4,1)S(1)}, s32[]{:S(2)}) async-start(s8[8388608]{0:T(1024)(128)(4,1)} %bitcast.53), calls=%async_computation.10 | async-start | bytes 8388608
  388.9 11.8 %slice-start.1 = ((s8[8388608]{0:T(1024)(128)(4,1)}), s8[4194304]{0:T(1024)(128)(4,1)S(1)}, s32[]{:S(2)}) async-start(s8[8388608]{0:T(1024)(128)(4,1)} %bitcast.53), calls=%async_computation.11 | async-start | bytes 8388608
  388.9 11.8 %copy-start = (bf16[1,1,2048,1024]{3,2,1,0:T(8,128)(2,1)S(1)}, bf16[1,1,2048,1024]{3,2,1,0:T(8,128)(2,1)}, u32[]{:S(2)}) copy-start(bf16[1,1,2048,1024]{3,2,1,0:T(8,128)(2,1)} %param.7) | copy-start | bytes 12582916
Sparse Core Ops, SparseCore 0:
  9.5 11.7 all-gather.3
  32.6 68.9 reduce-scatter.2
  104.0 22.1 all-reduce.4
  128.4 49.2 all-gather.5
  181.9 87.2 all-reduce.6
  272.0 9.1 reduce-scatter.4
  305.3 30.7 all-reduce.8
  337.7 9.2 all-gather.7

commit v2 on v1

v2 whole, which is shorter than its diff:
```python
import functools
import math

import jax
import jax.numpy as jnp
from jax import lax
from jax.experimental import pallas as pl
from jax.experimental.pallas import tpu as pltpu
from jax.sharding import PartitionSpec as P

highest = lax.Precision.HIGHEST
step_size = 0.3
drop_share = 0.05
guard_term = 1e-06
MESH = pl.DeviceIdType.MESH
PANEL = 32


def contract(left, right, left_dim, right_dim):
    return lax.dot_general(
        left,
        right,
        (((left_dim,), (right_dim,)), ((), ())),
        precision=highest,
        preferred_element_type=jnp.float32,
    )


def factor(aug):
    rank = aug.shape[0]

    @pl.loop(0, rank // PANEL)
    def _(block):
        first = pl.multiple_of(block * PANEL, PANEL)
        row = lax.broadcasted_iota(jnp.int32, (PANEL, 1), 0)
        lane = lax.broadcasted_iota(jnp.int32, (PANEL, rank), 1)

        def eliminate(step, work):
            column = jnp.sum(jnp.where(lane == first + step, work[:, :rank], 0.0), axis=1, keepdims=True)
            pivot = jnp.sum(jnp.where(row == step, column, 0.0), axis=0, keepdims=True)
            root = lax.rsqrt(pivot)
            line = jnp.sum(jnp.where(row == step, work, 0.0), axis=0, keepdims=True) * root
            rest = work - jnp.where(row > step, column * root, 0.0) * line
            return jnp.where(row == step, line, rest)

        work = lax.fori_loop(0, PANEL, eliminate, aug[pl.ds(first, PANEL), :])
        aug[pl.ds(first, PANEL), :] = work
        below = jnp.where(lane >= first + PANEL, work[:, :rank], 0.0)
        aug[...] -= contract(below, work, 0, 0)


def kernel(
    n, momentum, right_basis, gradients, other, left_out, coef_out, scaled_out,
    grad_in, share, grad, basis, part, part_in, own, own_in, sketch,
    gram_part, gram_in, gram_sum, gram_pair, gram_all, aug, left,
    coef_part, coef_in, coef_sum, coef_pair, coef_all, norm_own, norm_in, scale_own, scale_in,
    load_sem, grad_send, grad_recv, pair_send, pair_recv,
    part_send, part_recv, row_send, row_recv, gram_send, gram_recv,
    gall_send, gall_recv, norm_send, norm_recv, base_sem,
):
    dp, core, me = lax.axis_index("dp"), lax.axis_index("fsdp"), lax.axis_index("tensor")
    rows, _ = share.shape
    piece = rows // n
    half = right_basis.shape[0]
    rank = 2 * half
    lines = rank // n

    def at(index):
        return pl.ds(pl.multiple_of(index * piece, piece), piece)

    def load(index, slot):
        return (
            pltpu.make_async_copy(gradients.at[at(index)], grad_in.at[at(index)], load_sem.at[0, slot]),
            pltpu.make_async_copy(momentum.at[at(index)], share.at[at(index)], load_sem.at[1, slot]),
        )

    base = pltpu.make_async_copy(right_basis, basis.at[core], base_sem)
    base.start()

    @pl.loop(0, n)
    def _(k):
        for copy in load(lax.rem(me + k + 1, n), k):
            copy.start()

    barrier = pltpu.get_barrier_semaphore()
    pl.semaphore_signal(barrier, inc=1, device_id={"dp": 1 - dp}, device_id_type=MESH)
    pl.semaphore_signal(barrier, inc=1, device_id={"fsdp": 1 - core}, device_id_type=MESH)

    @pl.loop(1, n)
    def _(k):
        pl.semaphore_signal(barrier, inc=1, device_id={"tensor": lax.rem(me + k, n)}, device_id_type=MESH)

    pl.semaphore_wait(barrier, n + 1)

    def remote(src, dst, send, recv, where):
        return pltpu.make_async_remote_copy(
            src_ref=src, dst_ref=dst, send_sem=send, recv_sem=recv, device_id=where, device_id_type=MESH
        )

    def pair(index, src, dst, axis):
        where = {axis: 1 - (dp if axis == "dp" else core)}
        return remote(src, dst, pair_send.at[index], pair_recv.at[index], where)

    def grad_copy(k):
        index = lax.rem(me + k + 1, n)
        return remote(grad.at[at(index)], other.at[at(index)], grad_send.at[k], grad_recv.at[k], {"dp": 1 - dp})

    def send_grads(begin, end):
        @pl.loop(begin, end)
        def _(k):
            grad_copy(k).start()

    base.wait()
    basis_copy = pair(0, basis.at[core], basis.at[core], "fsdp")
    basis_copy.start()
    stages = [n * i // 8 for i in (3, 5, 6, 7, 8)]

    @pl.loop(0, n)
    def _(k):
        index = lax.rem(me + k + 1, n)
        for copy in load(index, k):
            copy.wait()
        value = grad_in[at(index), :].astype(jnp.float32)
        grad[at(index), :] = value
        share[at(index), :] = share[at(index), :] * 0.5 + value

        @pl.when(k < stages[0])
        def _():
            grad_copy(k).start()

    basis_copy.wait()

    def part_copy(k):
        return remote(
            part.at[lax.rem(me + k, n)], part_in.at[k], part_send.at[k], part_recv.at[k],
            {"tensor": lax.rem(me + k, n)},
        )

    @pl.loop(1, n + 1)
    def _(k):
        index = lax.rem(me + k, n)
        value = share[at(index), :]
        for h in range(2):
            part[index, :, h * half : (h + 1) * half] = contract(value, basis[h], 1, 1)

        @pl.when(k < n)
        def _():
            part_copy(k).start()

    own[...] = part[me]

    @pl.loop(1, n)
    def _(k):
        part_copy(k).wait()
        own[...] += part_in[k]

    dp_copy = pair(1, own, own_in, "dp")
    dp_copy.start()
    send_grads(stages[0], stages[1])
    dp_copy.wait()
    sketch[at(me), :] = own[...] + own_in[...]

    block = sketch[at(me), :]
    gram = contract(block, block, 0, 0)
    for i in range(n):
        gram_part[i] = gram[i * lines : (i + 1) * lines, :]

    def gram_copy(k):
        return remote(
            gram_part.at[lax.rem(me + k, n)], gram_in.at[k], gram_send.at[k], gram_recv.at[k],
            {"tensor": lax.rem(me + k, n)},
        )

    @pl.loop(1, n)
    def _(k):
        gram_copy(k).start()

    gram_sum[...] = gram_part[me]

    @pl.loop(1, n)
    def _(k):
        gram_copy(k).wait()
        gram_sum[...] += gram_in[k]

    gram_swap = pair(2, gram_sum, gram_pair, "fsdp")
    gram_swap.start()
    gram_swap.wait()
    gram_all[me] = gram_sum[...] + gram_pair[...]

    def gall_copy(k):
        return remote(
            gram_all.at[me], gram_all.at[me], gall_send.at[k], gall_recv.at[k], {"tensor": lax.rem(me + k, n)}
        )

    def row_copy(k):
        return remote(
            sketch.at[at(me)], sketch.at[at(me)], row_send.at[k], row_recv.at[k], {"tensor": lax.rem(me + k, n)}
        )

    def gall_arrival(k):
        source = lax.rem(me + n - k, n)
        return remote(
            gram_all.at[source], gram_all.at[source], gall_send.at[k], gall_recv.at[k],
            {"tensor": lax.rem(me + k, n)},
        )

    def row_arrival(k):
        source = lax.rem(me + n - k, n)
        return remote(
            sketch.at[at(source)], sketch.at[at(source)], row_send.at[k], row_recv.at[k],
            {"tensor": lax.rem(me + k, n)},
        )

    @pl.loop(1, n)
    def _(k):
        gall_copy(k).start()

    @pl.loop(1, n)
    def _(k):
        row_copy(k).start()

    send_grads(stages[1], stages[2])

    @pl.loop(1, n)
    def _(k):
        gall_copy(k).wait_send()
        gall_arrival(k).wait_recv()

    for i in range(n):
        aug[i * lines : (i + 1) * lines, :rank] = gram_all[i]
    diagonal = lax.broadcasted_iota(jnp.int32, (rank, rank), 0) == lax.broadcasted_iota(jnp.int32, (rank, rank), 1)
    aug[:, rank:] = jnp.where(diagonal, 1.0, 0.0)
    factor(aug)
    send_grads(stages[2], stages[3])

    @pl.loop(1, n)
    def _(k):
        row_copy(k).wait_send()
        row_arrival(k).wait_recv()

    coef_part[...] = jnp.zeros_like(coef_part)

    @pl.loop(0, n)
    def _(k):
        block = sketch[at(k), :]
        for h in range(2):
            value = contract(block, aug[h * half : (h + 1) * half, rank:], 1, 1)
            left[h, at(k), :] = value
            left_out[at(k), h * half : (h + 1) * half] = value

    def accumulate(h):
        @pl.loop(0, n)
        def _(k):
            coef_part[h] += contract(left[h, at(k), :], share[at(k), :], 0, 0)

    accumulate(1 - core)
    coef_swap = pair(3, coef_part.at[1 - core], coef_in, "fsdp")
    coef_swap.start()
    accumulate(core)
    coef_swap.wait()
    coef_sum[...] = coef_part[core] + coef_in[...]
    coef_dp = pair(4, coef_sum, coef_pair, "dp")
    coef_dp.start()
    send_grads(stages[3], stages[4])
    coef_dp.wait()
    coef_all[core] = coef_sum[...] + coef_pair[...]
    coef_share = pair(5, coef_all.at[core], coef_all.at[core], "fsdp")
    coef_share.start()

    value = coef_all[core]
    norm_own[...] = contract(jnp.ones((8, value.shape[1]), jnp.float32), value * value, 1, 1)

    def norm_copy(k):
        return remote(
            norm_own, norm_in.at[me], norm_send.at[k], norm_recv.at[k], {"tensor": lax.rem(me + k, n)}
        )

    def norm_arrival(k):
        source = lax.rem(me + n - k, n)
        return remote(
            norm_own, norm_in.at[source], norm_send.at[k], norm_recv.at[k], {"tensor": lax.rem(me + k, n)}
        )

    @pl.loop(1, n)
    def _(k):
        norm_copy(k).start()

    norm_in[me] = norm_own[...]

    @pl.loop(1, n)
    def _(k):
        norm_copy(k).wait_send()
        norm_arrival(k).wait_recv()

    total = norm_in[0]
    for i in range(1, n):
        total = total + norm_in[i]
    scale_own[...] = lax.rsqrt(total + guard_term)
    scale_copy = pair(6, scale_own, scale_in, "fsdp")
    scale_copy.start()
    scale_copy.wait()
    coef_share.wait()

    def scaled(h, scale):
        column = jnp.transpose(jnp.broadcast_to(scale[0:1, :], (half, half)))[:, 0:1]
        scaled_out[h] = coef_all[h] * column

    scaled(core, scale_own[...])
    scaled(1 - core, scale_in[...])
    coef_out[...] = coef_all[...]

    @pl.loop(0, n)
    def _(k):
        grad_copy(k).wait()


def exchange(n, momentum, right_basis, gradient):
    rows, cols = momentum.shape
    half = right_basis.shape[0]
    rank = 2 * half
    piece, lines = rows // n, rank // n
    f32 = jnp.float32
    vmem = pltpu.VMEM
    dma = pltpu.SemaphoreType.DMA
    any_spec = pl.BlockSpec(memory_space=pl.ANY)
    vmem_spec = pl.BlockSpec(memory_space=pltpu.VMEM)
    return pl.pallas_call(
        functools.partial(kernel, n),
        out_shape=(
            jax.ShapeDtypeStruct((rows, cols), f32),
            jax.ShapeDtypeStruct((rows, rank), f32),
            jax.ShapeDtypeStruct((2, half, cols), f32),
            jax.ShapeDtypeStruct((2, half, cols), f32),
        ),
        in_specs=[any_spec] * 3,
        out_specs=(any_spec, vmem_spec, vmem_spec, vmem_spec),
        scratch_shapes=[
            vmem((rows, cols), gradient.dtype),
            vmem((rows, cols), f32),
            vmem((rows, cols), f32),
            vmem((2, half, cols), f32),
            vmem((n, piece, rank), f32),
            vmem((n, piece, rank), f32),
            vmem((piece, rank), f32),
            vmem((piece, rank), f32),
            vmem((rows, rank), f32),
            vmem((n, lines, rank), f32),
            vmem((n, lines, rank), f32),
            vmem((lines, rank), f32),
            vmem((lines, rank), f32),
            vmem((n, lines, rank), f32),
            vmem((rank, 2 * rank), f32),
            vmem((2, rows, half), f32),
            vmem((2, half, cols), f32),
            vmem((half, cols), f32),
            vmem((half, cols), f32),
            vmem((half, cols), f32),
            vmem((2, half, cols), f32),
            vmem((8, half), f32),
            vmem((n, 8, half), f32),
            vmem((8, half), f32),
            vmem((8, half), f32),
            dma((2, n)), dma((n,)), dma((n,)), dma((7,)), dma((7,)),
            dma((n,)), dma((n,)), dma((n,)), dma((n,)), dma((n,)), dma((n,)),
            dma((n,)), dma((n,)), dma((n,)), dma((n,)), dma,
        ],
        compiler_params=pltpu.CompilerParams(
            collective_id=0, has_side_effects=True, vmem_limit_bytes=56 * 1024 * 1024
        ),
        cost_estimate=pl.CostEstimate(
            flops=6 * rows * cols * rank, bytes_accessed=20 * rows * cols, transcendentals=0
        ),
    )(momentum, right_basis, gradient)


def shards(n, step_scale, weight, momentum, right_basis, gradients):
    half, cols = right_basis.shape
    gradient = gradients[0, 0]
    other, left_basis, coefficients, scaled = exchange(n, momentum, right_basis, gradient)
    flat = scaled.reshape(2 * half, cols)
    weight = weight - step_scale * contract(left_basis, flat, 1, 0)
    total = momentum + (gradient.astype(jnp.float32) + other)
    momentum = total - drop_share * contract(left_basis, coefficients.reshape(2 * half, cols), 1, 0)
    first_rank = lax.axis_index("fsdp") * half
    return weight, momentum, lax.dynamic_slice_in_dim(flat, first_rank, half, 0)


def solution(mesh):
    assert mesh.shape["dp"] == 2 and mesh.shape["fsdp"] == 2
    n = mesh.shape["tensor"]

    def step(weight, momentum, right_basis, gradients):
        rows, width = weight.shape
        step_scale = step_size * math.sqrt(rows * width / right_basis.shape[0])
        return jax.shard_map(
            functools.partial(shards, n, step_scale),
            mesh=mesh,
            in_specs=(
                P("fsdp", "tensor"),
                P("fsdp", "tensor"),
                P("fsdp", "tensor"),
                P(None, "dp", "fsdp", "tensor"),
            ),
            out_specs=(P("fsdp", "tensor"), P("fsdp", "tensor"), P("fsdp", "tensor")),
            check_vma=False,
        )(weight, momentum, right_basis, gradients)

    return step
```

time: 420 us -> 236 us (0.56)
  waiting for transfers between devices: 258 us -> 0 us
  Pallas kernels: 0 us -> 208 us
  other arithmetic: 61.5 us -> 0 us
  matrix products: 56 us -> 26.6 us
  blocking collectives: 21.4 us -> 0 us
  between operations: 15.6 us -> 0.67 us
  local copies, waits for them, and re-layouts: 5.98 us -> 0.84 us
    pallas_call x0 -> x1, Pallas kernels: none -> 208 us  [exchange(): pl.pallas_call(functools.partial(kernel, n), out_shape=(jax.ShapeDtypeStr...]
    psum x3 -> x0, waiting for transfers between devices: 132 us -> none  [the longest x1 78.8 us: shards(): gram = lax.psum(contract(block, block, 0, 0), ('tensor', 'fsdp'))]
    reduce_scatter x2 -> x0, waiting for transfers between devices: 69.1 us -> none  [the longest x1 69.1 us: shards(): block = lax.psum_scatter(part, 'tensor', scatter_dimension=0, tiled=True)]
    all_gather x3 -> x0, waiting for transfers between devices: 56.5 us -> none  [the longest x1 43.1 us: shards(): sketch = lax.all_gather(block, 'tensor', axis=0, tiled=True)]
    another operation x9 -> x0, other arithmetic: 53.7 us -> none  [the longest x6 33.9 us: inverse_factor(): lower = jnp.linalg.cholesky(gram)]
    dot_general x7 -> x2, matrix products: 54.7 us -> 26.6 us  [contract(): lax.dot_general(left, right, (((left_dim,), (right_dim,)), ((), ())), pre...]
    psum x1 -> x0, blocking collectives: 21.4 us -> none  [shards(): squares = lax.psum(jnp.sum(coefficients * coefficients, axis=1), 'tensor')]
    convert_element_type x1 -> x0, other arithmetic: 6.67 us -> none  [shards(): gradient = gradients[0, 0].astype(jnp.float32)]
  transfers between devices with their start and end apart: 9 -> 0, of which waited for: 6 -> 0; matrix products, arithmetic and copies ran while one was open for 24% -> 0% of each run, Pallas kernels for 0% -> 0%
where the time goes in v2:
time: 236 us
  Pallas kernels  208 us (88%)
  matrix products  26.6 us (11%)
    pallas_call x1, Pallas kernels, exchange(): pl.pallas_call(functools.partial(kernel, n), out_shape=(jax.ShapeDtypeStr...  208 us
    dot_general x2, matrix products, contract(): lax.dot_general(left, right, (((left_dim,), (right_dim,)), ((), ())), pre...  26.6 us

profile of v2, /device:TPU:0, one launch (start us, length us, event | category | flops | bytes accessed | tf_op | source)
XLA Modules:
  0.0 236.1 jit_solution(13798583797382797243)
XLA Ops:
  0.6 0.0 copy-start
  0.6 208.0 %shard_map.67 = (f32[2048,1024]{1,0:T(8,128)}, f32[2048,256]{1,0:T(8,128)}, f32[2,128,1024]{2,1,0:T(8,128)}, f32[2,128,1024]{2,1,0:T(8,128)}) custom-call(f32[2048,1024]{1,0:T(8,128)} %momentum.1, f32[128,1024]{1,0:T(8,128)} %right_basis.1, bf16[2048,1024]{1,0:T(8,128)(2,1)} %bitcast.8), custom_call_target="tpu_custom_call" | custom-call | flops 3221225472 | bytes 41943040 | tf_op jit(solution)/shard_map/pallas_call | solution.py:327
  208.7 0.0 copy-done
  208.7 0.0 copy-start.2
  208.7 0.0 copy-start.1
  208.7 15.4 %multiply_subtract_fusion = f32[2048,1024]{1,0:T(8,128)} fusion(f32[2048,1024]{1,0:T(8,128)} %momentum.1, f32[2048,1024]{1,0:T(8,128)} %get-tuple-element.9, f32[2048,256]{1,0:T(8,128)} %get-tuple-element.7, f32[256,1024]{1,0:T(8,128)} %bitcast.11, bf16[1,1,2048,1024]{3,2,1,0:T(8,128)(2,1)S(1)} %copy-done), kind=kOutput, calls=%fused_computation | convolution fusion | flops 6452936704 | bytes 32505856 | tf_op jit(solution)/shard_map/dot_general | solution.py:20
  224.1 0.0 copy-done.2
  224.1 0.8 constant_dynamic-slice_fusion
  224.9 0.0 copy-done.1
  224.9 11.2 %multiply_subtract_fusion.1 = f32[2048,1024]{1,0:T(8,128)} fusion(f32[2048,1024]{1,0:T(8,128)} %param.4, f32[2048,256]{1,0:T(8,128)S(1)} %copy-done.1, f32[256,1024]{1,0:T(8,128)S(1)} %bitcast.10), kind=kOutput, calls=%fused_computation.1 | convolution fusion | flops 6446645248 | bytes 19922944 | tf_op jit(solution)/shard_map/dot_general | solution.py:20
Async XLA Ops:
  0.6 208.0 %copy-start = (bf16[1,1,2048,1024]{3,2,1,0:T(8,128)(2,1)S(1)}, bf16[1,1,2048,1024]{3,2,1,0:T(8,128)(2,1)}, u32[]{:S(2)}) copy-start(bf16[1,1,2048,1024]{3,2,1,0:T(8,128)(2,1)} %param.7) | copy-start | bytes 12582916
  208.7 15.4 %copy-start.2 = (f32[2,128,1024]{2,1,0:T(8,128)S(1)}, f32[2,128,1024]{2,1,0:T(8,128)}, u32[]{:S(2)}) copy-start(f32[2,128,1024]{2,1,0:T(8,128)} %get-tuple-element.8) | copy-start | bytes 3145732
  208.7 16.2 %copy-start.1 = (f32[2048,256]{1,0:T(8,128)S(1)}, f32[2048,256]{1,0:T(8,128)}, u32[]{:S(2)}) copy-start(f32[2048,256]{1,0:T(8,128)} %get-tuple-element.7) | copy-start | bytes 6291460

commit v3 on v2

--- a/solution.py
+++ b/solution.py
@@ -50,13 +50,13 @@
 
 
 def kernel(
-    n, momentum, right_basis, gradients, other, left_out, coef_out, scaled_out,
-    grad_in, share, grad, basis, part, part_in, own, own_in, sketch,
+    n, momentum, right_basis, gradients, total_out, left_out, coef_out, scaled_out,
+    grad_in, share, grad, other, basis, part, part_in, own, own_in, sketch,
     gram_part, gram_in, gram_sum, gram_pair, gram_all, aug, left,
     coef_part, coef_in, coef_sum, coef_pair, coef_all, norm_own, norm_in, scale_own, scale_in,
     load_sem, grad_send, grad_recv, pair_send, pair_recv,
     part_send, part_recv, row_send, row_recv, gram_send, gram_recv,
-    gall_send, gall_recv, norm_send, norm_recv, base_sem,
+    gall_send, gall_recv, norm_send, norm_recv, total_sem, base_sem,
 ):
     dp, core, me = lax.axis_index("dp"), lax.axis_index("fsdp"), lax.axis_index("tensor")
     rows, _ = share.shape
@@ -68,10 +68,13 @@
     def at(index):
         return pl.ds(pl.multiple_of(index * piece, piece), piece)
 
+    def load_momentum(index, slot):
+        return pltpu.make_async_copy(momentum.at[at(index)], share.at[at(index)], load_sem.at[1, slot])
+
     def load(index, slot):
         return (
             pltpu.make_async_copy(gradients.at[at(index)], grad_in.at[at(index)], load_sem.at[0, slot]),
-            pltpu.make_async_copy(momentum.at[at(index)], share.at[at(index)], load_sem.at[1, slot]),
+            load_momentum(index, slot),
         )
 
     base = pltpu.make_async_copy(right_basis, basis.at[core], base_sem)
@@ -113,7 +116,7 @@
     base.wait()
     basis_copy = pair(0, basis.at[core], basis.at[core], "fsdp")
     basis_copy.start()
-    stages = [n * i // 8 for i in (3, 5, 6, 7, 8)]
+    stages = [n * i // 8 for i in (4, 6, 7, 8, 8)]
 
     @pl.loop(0, n)
     def _(k):
@@ -257,6 +260,11 @@
     coef_swap = pair(3, coef_part.at[1 - core], coef_in, "fsdp")
     coef_swap.start()
     accumulate(core)
+
+    @pl.loop(0, n)
+    def _(k):
+        load_momentum(lax.rem(me + k + 1, n), k).start()
+
     coef_swap.wait()
     coef_sum[...] = coef_part[core] + coef_in[...]
     coef_dp = pair(4, coef_sum, coef_pair, "dp")
@@ -309,9 +317,59 @@
     scaled(1 - core, scale_in[...])
     coef_out[...] = coef_all[...]
 
-    @pl.loop(0, n)
-    def _(k):
+    def total_copy(k):
+        index = lax.rem(me + k + 1, n)
+        return pltpu.make_async_copy(other.at[at(index)], total_out.at[at(index)], total_sem.at[k])
+
+    @pl.loop(0, n)
+    def _(k):
+        index = lax.rem(me + k + 1, n)
+        load_momentum(index, k).wait()
         grad_copy(k).wait()
+        other[at(index), :] = share[at(index), :] + (grad[at(index), :] + other[at(index), :])
+        total_copy(k).start()
+
+    @pl.loop(0, n)
+    def _(k):
+        total_copy(k).wait()
+
+
+def split(value):
+    high = value.astype(jnp.bfloat16)
+    return high, (value - high.astype(jnp.float32)).astype(jnp.bfloat16)
+
+
+def finish(step_scale, left, coefficients, scaled, total, weight, weight_out, momentum_out, coef_parts, scaled_parts):
+    @pl.when(pl.program_id(0) == 0)
+    def _():
+        for source, parts in ((coefficients, coef_parts), (scaled, scaled_parts)):
+            high, low = split(source[...])
+            parts[...] = jnp.concatenate([high, low, high], axis=0)
+
+    high, low = split(left[...])
+    lefts = jnp.concatenate([high, high, low], axis=1)
+    momentum_out[...] = total[...] - drop_share * jnp.dot(lefts, coef_parts[...], preferred_element_type=jnp.float32)
+    weight_out[...] = weight[...] - step_scale * jnp.dot(lefts, scaled_parts[...], preferred_element_type=jnp.float32)
+
+
+def update(step_scale, left, coefficients, scaled, total, weight):
+    rows, cols = weight.shape
+    rank = coefficients.shape[0]
+    tile = math.gcd(rows, 128)
+    wide = pl.BlockSpec((tile, cols), lambda i: (i, 0))
+    whole = pl.BlockSpec((rank, cols), lambda i: (0, 0))
+    return pl.pallas_call(
+        functools.partial(finish, step_scale),
+        grid=(rows // tile,),
+        out_shape=(jax.ShapeDtypeStruct(weight.shape, weight.dtype),) * 2,
+        in_specs=[pl.BlockSpec((tile, rank), lambda i: (i, 0)), whole, whole, wide, wide],
+        out_specs=(wide, wide),
+        scratch_shapes=[pltpu.VMEM((3 * rank, cols), jnp.bfloat16)] * 2,
+        compiler_params=pltpu.CompilerParams(vmem_limit_bytes=60 * 1024 * 1024),
+        cost_estimate=pl.CostEstimate(
+            flops=12 * rows * cols * rank, bytes_accessed=18 * rows * cols, transcendentals=0
+        ),
+    )(left, coefficients, scaled, total, weight)
 
 
 def exchange(n, momentum, right_basis, gradient):
@@ -336,6 +394,7 @@
         out_specs=(any_spec, vmem_spec, vmem_spec, vmem_spec),
         scratch_shapes=[
             vmem((rows, cols), gradient.dtype),
+            vmem((rows, cols), f32),
             vmem((rows, cols), f32),
             vmem((rows, cols), f32),
             vmem((2, half, cols), f32),
@@ -362,7 +421,7 @@
             vmem((8, half), f32),
             dma((2, n)), dma((n,)), dma((n,)), dma((7,)), dma((7,)),
             dma((n,)), dma((n,)), dma((n,)), dma((n,)), dma((n,)), dma((n,)),
-            dma((n,)), dma((n,)), dma((n,)), dma((n,)), dma,
+            dma((n,)), dma((n,)), dma((n,)), dma((n,)), dma((n,)), dma,
         ],
         compiler_params=pltpu.CompilerParams(
             collective_id=0, has_side_effects=True, vmem_limit_bytes=56 * 1024 * 1024
@@ -375,12 +434,11 @@
 
 def shards(n, step_scale, weight, momentum, right_basis, gradients):
     half, cols = right_basis.shape
-    gradient = gradients[0, 0]
-    other, left_basis, coefficients, scaled = exchange(n, momentum, right_basis, gradient)
+    total, left_basis, coefficients, scaled = exchange(n, momentum, right_basis, gradients[0, 0])
     flat = scaled.reshape(2 * half, cols)
-    weight = weight - step_scale * contract(left_basis, flat, 1, 0)
-    total = momentum + (gradient.astype(jnp.float32) + other)
-    momentum = total - drop_share * contract(left_basis, coefficients.reshape(2 * half, cols), 1, 0)
+    weight, momentum = update(
+        step_scale, left_basis, coefficients.reshape(2 * half, cols), flat, total, weight
+    )
     first_rank = lax.axis_index("fsdp") * half
     return weight, momentum, lax.dynamic_slice_in_dim(flat, first_rank, half, 0)
 

time: 236 us -> 239 us (1.013)
  Pallas kernels: 208 us -> 237 us
  matrix products: 26.6 us -> 0 us
    dot_general x2 -> x0, matrix products: 26.6 us -> none  [contract(): lax.dot_general(left, right, (((left_dim,), (right_dim,)), ((), ())), pre...]
    pallas_call x0 -> x1, Pallas kernels: none -> 20.7 us  [update(): pl.pallas_call(functools.partial(finish, step_scale), grid=(rows // tile,...]
    pallas_call x1, Pallas kernels: 208 us -> 216 us  [exchange(): pl.pallas_call(functools.partial(kernel, n), out_shape=(jax.ShapeDtypeStr...]
where the time goes in v3:
time: 239 us
  Pallas kernels  237 us (99%)
    pallas_call x1, Pallas kernels, exchange(): pl.pallas_call(functools.partial(kernel, n), out_shape=(jax.ShapeDtypeStr...  216 us
    pallas_call x1, Pallas kernels, update(): pl.pallas_call(functools.partial(finish, step_scale), grid=(rows // tile,...  20.7 us

profile of v3, /device:TPU:0, one launch (start us, length us, event | category | flops | bytes accessed | tf_op | source)
XLA Modules:
  0.0 238.7 jit_solution(13647917613812537751)
XLA Ops:
  0.6 216.4 %shard_map.67 = (f32[2048,1024]{1,0:T(8,128)}, f32[2048,256]{1,0:T(8,128)}, f32[2,128,1024]{2,1,0:T(8,128)}, f32[2,128,1024]{2,1,0:T(8,128)}) custom-call(f32[2048,1024]{1,0:T(8,128)} %momentum.1, f32[128,1024]{1,0:T(8,128)} %right_basis.1, bf16[2048,1024]{1,0:T(8,128)(2,1)} %bitcast.3), custom_call_target="tpu_custom_call" | custom-call | flops 3221225472 | bytes 41943040 | tf_op jit(solution)/shard_map/pallas_call | solution.py:385
  217.1 0.0 copy-start
  217.1 20.7 %shard_map.68 = (f32[2048,1024]{1,0:T(8,128)}, f32[2048,1024]{1,0:T(8,128)}) custom-call(f32[2048,256]{1,0:T(8,128)} %get-tuple-element.9.left, f32[256,1024]{1,0:T(8,128)} %bitcast.6, f32[256,1024]{1,0:T(8,128)} %bitcast.4, f32[2048,1024]{1,0:T(8,128)} %get-tuple-element.12.total, f32[2048,1024]{1,0:T(8,128)} %weight.1), custom_call_target="tpu_custom_call" | custom-call | flops 6442450944 | bytes 37748736 | tf_op jit(solution)/shard_map/pallas_call | solution.py:361
  237.8 0.0 copy-done
  237.8 0.8 constant_dynamic-slice_fusion
Async XLA Ops:
  217.1 20.7 %copy-start = (f32[2,128,1024]{2,1,0:T(8,128)S(1)}, f32[2,128,1024]{2,1,0:T(8,128)}, u32[]{:S(2)}) copy-start(f32[2,128,1024]{2,1,0:T(8,128)} %get-tuple-element.11) | copy-start | bytes 3145732

commit v4 on v3

--- a/solution.py
+++ b/solution.py
@@ -116,7 +116,7 @@
     base.wait()
     basis_copy = pair(0, basis.at[core], basis.at[core], "fsdp")
     basis_copy.start()
-    stages = [n * i // 8 for i in (4, 6, 7, 8, 8)]
+    stages = [n * i // 8 for i in (3, 5, 6, 7, 8)]
 
     @pl.loop(0, n)
     def _(k):
@@ -355,7 +355,7 @@
 def update(step_scale, left, coefficients, scaled, total, weight):
     rows, cols = weight.shape
     rank = coefficients.shape[0]
-    tile = math.gcd(rows, 128)
+    tile = math.gcd(rows, 256)
     wide = pl.BlockSpec((tile, cols), lambda i: (i, 0))
     whole = pl.BlockSpec((rank, cols), lambda i: (0, 0))
     return pl.pallas_call(

time: 239 us -> 228 us (0.954)
  Pallas kernels: 237 us -> 226 us
    pallas_call x1, Pallas kernels: 216 us -> 209 us  [exchange(): pl.pallas_call(functools.partial(kernel, n), out_shape=(jax.ShapeDtypeStr...]
    pallas_call x1, Pallas kernels: 20.7 us -> 17.2 us  [update(): pl.pallas_call(functools.partial(finish, step_scale), grid=(rows // tile,...]
where the time goes in v4:
time: 228 us
  Pallas kernels  226 us (99%)
    pallas_call x1, Pallas kernels, exchange(): pl.pallas_call(functools.partial(kernel, n), out_shape=(jax.ShapeDtypeStr...  209 us
    pallas_call x1, Pallas kernels, update(): pl.pallas_call(functools.partial(finish, step_scale), grid=(rows // tile,...  17.2 us

profile of v4, /device:TPU:0, one launch (start us, length us, event | category | flops | bytes accessed | tf_op | source)
XLA Modules:
  0.0 227.9 jit_solution(15280602116520330394)
XLA Ops:
  0.6 209.1 %shard_map.67 = (f32[2048,1024]{1,0:T(8,128)}, f32[2048,256]{1,0:T(8,128)}, f32[2,128,1024]{2,1,0:T(8,128)}, f32[2,128,1024]{2,1,0:T(8,128)}) custom-call(f32[2048,1024]{1,0:T(8,128)} %momentum.1, f32[128,1024]{1,0:T(8,128)} %right_basis.1, bf16[2048,1024]{1,0:T(8,128)(2,1)} %bitcast.3), custom_call_target="tpu_custom_call" | custom-call | flops 3221225472 | bytes 41943040 | tf_op jit(solution)/shard_map/pallas_call | solution.py:385
  209.8 0.0 copy-start
  209.8 17.2 %shard_map.68 = (f32[2048,1024]{1,0:T(8,128)}, f32[2048,1024]{1,0:T(8,128)}) custom-call(f32[2048,256]{1,0:T(8,128)} %get-tuple-element.9.left, f32[256,1024]{1,0:T(8,128)} %bitcast.6, f32[256,1024]{1,0:T(8,128)} %bitcast.4, f32[2048,1024]{1,0:T(8,128)} %get-tuple-element.12.total, f32[2048,1024]{1,0:T(8,128)} %weight.1), custom_call_target="tpu_custom_call" | custom-call | flops 6442450944 | bytes 37748736 | tf_op jit(solution)/shard_map/pallas_call | solution.py:361
  227.0 0.0 copy-done
  227.0 0.8 constant_dynamic-slice_fusion
Async XLA Ops:
  209.8 17.3 %copy-start = (f32[2,128,1024]{2,1,0:T(8,128)S(1)}, f32[2,128,1024]{2,1,0:T(8,128)}, u32[]{:S(2)}) copy-start(f32[2,128,1024]{2,1,0:T(8,128)} %get-tuple-element.11) | copy-start | bytes 3145732

commit v5 on v4

--- a/solution.py
+++ b/solution.py
@@ -116,7 +116,7 @@
     base.wait()
     basis_copy = pair(0, basis.at[core], basis.at[core], "fsdp")
     basis_copy.start()
-    stages = [n * i // 8 for i in (3, 5, 6, 7, 8)]
+    stages = [n * i // 8 for i in (3, 5, 7, 7, 8)]
 
     @pl.loop(0, n)
     def _(k):
@@ -355,7 +355,7 @@
 def update(step_scale, left, coefficients, scaled, total, weight):
     rows, cols = weight.shape
     rank = coefficients.shape[0]
-    tile = math.gcd(rows, 256)
+    tile = math.gcd(rows, 512)
     wide = pl.BlockSpec((tile, cols), lambda i: (i, 0))
     whole = pl.BlockSpec((rank, cols), lambda i: (0, 0))
     return pl.pallas_call(

time: 228 us -> 226 us (level)
  no operation moved by 1% of the time
where the time goes in v5:
time: 226 us
  Pallas kernels  224 us (99%)
    pallas_call x1, Pallas kernels, exchange(): pl.pallas_call(functools.partial(kernel, n), out_shape=(jax.ShapeDtypeStr...  209 us
    pallas_call x1, Pallas kernels, update(): pl.pallas_call(functools.partial(finish, step_scale), grid=(rows // tile,...  15.3 us

profile of v5, /device:TPU:0, one launch (start us, length us, event | category | flops | bytes accessed | tf_op | source)
XLA Modules:
  0.0 225.9 jit_solution(10785967165569268070)
XLA Ops:
  0.6 209.1 %shard_map.67 = (f32[2048,1024]{1,0:T(8,128)}, f32[2048,256]{1,0:T(8,128)}, f32[2,128,1024]{2,1,0:T(8,128)}, f32[2,128,1024]{2,1,0:T(8,128)}) custom-call(f32[2048,1024]{1,0:T(8,128)} %momentum.1, f32[128,1024]{1,0:T(8,128)} %right_basis.1, bf16[2048,1024]{1,0:T(8,128)(2,1)} %bitcast.3), custom_call_target="tpu_custom_call" | custom-call | flops 3221225472 | bytes 41943040 | tf_op jit(solution)/shard_map/pallas_call | solution.py:385
  209.8 0.0 copy-start
  209.8 15.3 %shard_map.68 = (f32[2048,1024]{1,0:T(8,128)}, f32[2048,1024]{1,0:T(8,128)}) custom-call(f32[2048,256]{1,0:T(8,128)} %get-tuple-element.9.left, f32[256,1024]{1,0:T(8,128)} %bitcast.6, f32[256,1024]{1,0:T(8,128)} %bitcast.4, f32[2048,1024]{1,0:T(8,128)} %get-tuple-element.12.total, f32[2048,1024]{1,0:T(8,128)} %weight.1), custom_call_target="tpu_custom_call" | custom-call | flops 6442450944 | bytes 37748736 | tf_op jit(solution)/shard_map/pallas_call | solution.py:361
  225.0 0.0 copy-done
  225.1 0.8 constant_dynamic-slice_fusion
Async XLA Ops:
  209.8 15.3 %copy-start = (f32[2,128,1024]{2,1,0:T(8,128)S(1)}, f32[2,128,1024]{2,1,0:T(8,128)}, u32[]{:S(2)}) copy-start(f32[2,128,1024]{2,1,0:T(8,128)} %get-tuple-element.11) | copy-start | bytes 3145732
